TPU v7x, 128 devices: a whole 4x4x4 slice. The times are simulated.
128 devices in a mesh: band: 16 (over y, z), patch: 8 (over x, core).
Axes of the slice: x: 4, y: 4, z: 4, core: 2. Of those that a mesh axis runs over, the one named last changes fastest.
Arguments:
- grid_feat: bfloat16 [32768, 227], P(('band', 'patch')), may hold values from -6 to 6
- mesh_state: bfloat16 [32768, 512], P(('band', 'patch')), may hold values from -6 to 6
- g2m_dest: int32 [32768, 4], P(('band', 'patch')), may hold values from 0 to 127, all different within a row; in each aligned block of 256 rows (0 to 255, 256 to 511, ...) at most 16 rows name the same one
- g2m_node: int32 [32768, 4], P(('band', 'patch')), may hold values from 0 to 255
- g2m_dist: bfloat16 [32768, 4], P(('band', 'patch')), may hold values from 0.25 to 2
- mesh_src: int32 [32768, 6], P(('band', 'patch')), may hold values from 0 to 32767, as said below
- w_embed: bfloat16 [227, 512], replicated, may hold values from -0.375 to 0.375
- w_send: bfloat16 [512, 512], replicated, may hold values from -0.25 to 0.25
- w_recv: bfloat16 [512, 512], replicated, may hold values from -0.25 to 0.25
- w_node: bfloat16 [512, 512], replicated, may hold values from -0.25 to 0.25
- edge_vec: bfloat16 [512], replicated, may hold values from -4 to 4
- proc_weights: bfloat16 [2, 3, 512, 512], replicated, may hold values from -0.25 to 0.25
- cotangent: bfloat16 [32768, 512], P(('band', 'patch')), may hold values from -6 to 6
Outputs:
- mesh_out: bfloat16 [32768, 512], P(('band', 'patch'))
- mesh_grad: bfloat16 [32768, 512], P(('band', 'patch'))
- grid_grad: bfloat16 [32768, 227], P(('band', 'patch'))
Inputs may be any that keep to these rules, and one draw needn't show every extreme that they name: `g2m_dest`: among the 256 grid nodes of one device's block, no device is named by more than 16 edges, and in every draw some device is named by exactly 16. The 4 devices of one grid node differ. `mesh_src`: the sender of an edge into a mesh node of device (b, p) lies on device (b, p), or among the last 128 mesh nodes of device (b, p - 1), or among the first 128 of device (b, p + 1), patch indices taken modulo 8.
All inputs are finite; a program needn't handle non-finite values.
Results may differ from a plain program's by a relative error of at most 0.023.
Values may be sent and summed in bfloat16 or wider, within the bound.
A program may use at most 128 MiB of HBM per device.

v0:
```python
import jax
import jax.numpy as jnp
from jax import lax
from jax.sharding import PartitionSpec as P

TOP = 4
DEG = 6
RIM = 128
LAYERS = 2
CAP = 16
WIDE = 256
AXES = ("band", "patch")
F32 = jnp.float32
BF16 = jnp.bfloat16


def mm(left, right):
    return lax.dot_general(left, right, (((1,), (0,)), ((), ())), preferred_element_type=F32)


def mm_t(left, right):
    return lax.dot_general(left, right, (((1,), (1,)), ((), ())), preferred_element_type=F32)


def t_mm(left, right):
    return lax.dot_general(left, right, (((0,), (0,)), ((), ())), preferred_element_type=F32)


def act(value):
    sig = jax.nn.sigmoid(value)
    out = value * sig
    return out, sig + out * (1.0 - sig)


def shift(x, up):
    n = lax.axis_size("patch")
    return lax.ppermute(x, "patch", [(i, (i + (1 if up else -1)) % n) for i in range(n)])


def exchange(x):
    return lax.all_to_all(x, AXES, split_axis=0, concat_axis=0, tiled=True)


def local(grid_feat, mesh_state, g2m_dest, g2m_node, g2m_dist, mesh_src, w_embed, w_send, w_recv, w_node, edge_vec, proc_weights, cotangent):
    peers = lax.axis_size(AXES)
    patches = lax.axis_size("patch")
    rows, cin = grid_feat.shape
    nodes, width = mesh_state.shape
    slots = peers * CAP
    own = lax.axis_index(AXES)
    dest_t, node_t, dist_t = g2m_dest.T, g2m_node.T, g2m_dist.T

    peer_ids = jnp.arange(peers, dtype=jnp.int32)[:, None]
    named = sum([(dest_t[k][None, :] == peer_ids).astype(BF16) for k in range(TOP)])
    before = (jnp.arange(rows)[:, None] < jnp.arange(rows)[None, :]).astype(BF16)
    rank = mm(named, before)
    place = jnp.where(named > 0, rank, -1.0)
    pick = (
        (place[:, None, :] == jnp.arange(CAP, dtype=F32)[None, :, None]).astype(BF16).reshape(slots, rows)
    )
    spare = WIDE - cin - 3 * TOP
    packed = jnp.concatenate(
        [grid_feat, (g2m_dest + 1).astype(BF16), (g2m_node + 1).astype(BF16), g2m_dist, jnp.zeros((rows, spare), BF16)],
        axis=1,
    )
    sent = mm(pick, packed).astype(BF16)
    got = exchange(sent.reshape(peers, CAP, WIDE)).reshape(slots, WIDE)

    dest = got[:, cin : cin + TOP].astype(F32)
    mine = dest == (own + 1).astype(F32)
    node = jnp.sum(jnp.where(mine, got[:, cin + TOP : cin + 2 * TOP].astype(F32), 0.0), axis=1, keepdims=True)
    dist = jnp.sum(jnp.where(mine, got[:, cin + 2 * TOP : cin + 3 * TOP].astype(F32), 0.0), axis=1, keepdims=True)
    here = (node == jnp.arange(1, nodes + 1, dtype=F32)[None, :]).astype(BF16)
    w_embed_wide = jnp.concatenate([w_embed, jnp.zeros((WIDE - cin, width), BF16)], axis=0)

    latent, d_embed = act(mm(got, w_embed_wide))
    recv_proj = mm(mesh_state, w_recv).astype(BF16)
    enc_pre = mm(latent.astype(BF16), w_send) + mm(here, recv_proj) + dist * edge_vec.astype(F32)[None, :]
    enc, d_enc = act(enc_pre)
    aggregate = t_mm(here, enc.astype(BF16)).astype(BF16)
    upd, d_node = act(mm(aggregate, w_node))
    hidden = (mesh_state.astype(F32) + upd).astype(BF16)

    own_patch = own % patches
    src_dev = mesh_src // nodes
    src_local = mesh_src % nodes
    left_side = src_dev % patches == (own_patch + patches - 1) % patches
    ext_index = jnp.where(
        src_dev == own,
        RIM + src_local,
        jnp.where(left_side, src_local - (nodes - RIM), RIM + nodes + src_local),
    )
    wide = nodes + 2 * RIM
    chosen = (ext_index.T.reshape(-1)[:, None] == jnp.arange(wide)[None, :]).astype(BF16)
    saved = []
    for layer in range(LAYERS):
        w_s, w_r, w_a = [proc_weights[layer, i] for i in range(3)]
        ext = jnp.concatenate([shift(hidden[nodes - RIM :], True), hidden, shift(hidden[:RIM], False)], axis=0)
        send_p = mm(ext, w_s).astype(BF16)
        recv_p = mm(hidden, w_r)
        proc, d_proc = act(mm(chosen, send_p).reshape(DEG, nodes, width) + recv_p[None])
        mean_msg = (proc.sum(axis=0) / DEG).astype(BF16)
        upd, d_upd = act(mm(mean_msg, w_a))
        saved.append((d_proc, d_upd))
        hidden = (hidden.astype(F32) + upd).astype(BF16)
    grad = cotangent.astype(F32)
    for layer in reversed(range(LAYERS)):
        w_s, w_r, w_a = [proc_weights[layer, i] for i in range(3)]
        d_proc, d_upd = saved[layer]
        grad_mean = mm_t((grad * d_upd).astype(BF16), w_a) / DEG
        grad_pre = (grad_mean[None] * d_proc).astype(BF16)
        grad_recv = grad_pre.astype(F32).sum(axis=0).astype(BF16)
        grad_ext = t_mm(chosen, grad_pre.reshape(DEG * nodes, width))
        from_right = shift(grad_ext[:RIM].astype(BF16), False)
        from_left = shift(grad_ext[RIM + nodes :].astype(BF16), True)
        grad_send = grad_ext[RIM : RIM + nodes]
        grad_send = grad_send.at[:RIM].add(from_left.astype(F32)).at[nodes - RIM :].add(from_right.astype(F32))
        grad = grad + mm_t(grad_recv, w_r) + mm_t(grad_send.astype(BF16), w_s)
    grad_agg = mm_t((grad * d_node).astype(BF16), w_node).astype(BF16)
    grad_enc = (mm(here, grad_agg) * d_enc).astype(BF16)
    grad_rproj = t_mm(here, grad_enc).astype(BF16)
    mesh_grad = (grad + mm_t(grad_rproj, w_recv)).astype(BF16)
    grad_embed = (mm_t(grad_enc, w_send) * d_embed).astype(BF16)
    back = exchange(mm_t(grad_embed, w_embed_wide).astype(BF16).reshape(peers, CAP, WIDE)).reshape(slots, WIDE)
    grid_grad = t_mm(pick, back)[:, :cin].astype(BF16)
    return hidden, mesh_grad, grid_grad


def solution(mesh):
    split = P(AXES, None)
    return jax.shard_map(
        local,
        mesh=mesh,
        in_specs=(split,) * 6 + (P(),) * 6 + (split,),
        out_specs=(split,) * 3,
        check_vma=False,
    )
```

profile of v0, /device:TPU:1, one launch (start us, length us, event | category | flops | bytes accessed | tf_op | source)
XLA Modules:
  0.0 147.5 jit_solution(8013060838337415927)
XLA Ops:
  0.6 0.0 copy-start
  0.7 0.8 fusion.172
  1.5 0.7 add_convert_fusion.3
  2.2 0.1 eq.155
  2.3 0.2 convolution_select_fusion
  2.5 0.0 copy-start.7
  2.5 0.3 bitcast_compare_fusion
  2.9 1.8 %concatenate.20 = bf16[256,256]{0,1:T(8,128)(2,1)S(1)} concatenate(bf16[256,227]{0,1:T(8,128)(2,1)} %param.21, bf16[256,4]{0,1:T(4,128)(2,1)S(1)} %get-tuple-element.76, bf16[256,4]{0,1:T(4,128)(2,1)S(1)} %get-tuple-element.75, bf16[256,4]{0,1:T(4,128)(2,1)} %param.25, bf16[256,17]{0,1:T(8,128)(2,1)S(1)} %broadcast_in_dim.12), dimensions={1} | concatenate | bytes 262144 | tf_op jit(solution)/shard_map/concatenate | solution.py:62
  4.7 1.5 %convolution_convert_fusion.1 = bf16[2048,256]{1,0:T(8,128)(2,1)} fusion(pred[2048,256]{1,0:T(32,128)(4,1)S(1)} %bitcast_compare_fusion, bf16[256,256]{0,1:T(8,128)(2,1)S(1)} %concatenate.20), kind=kOutput, calls=%fused_computation.37 | convolution fusion | flops 268959744 | bytes 1703936 | tf_op jit(solution)/shard_map/dot_general | solution.py:18
  6.2 11.5 %all-to-all-start = ((bf16[128,16,256]{2,1,0:T(8,128)(2,1)}), bf16[128,16,256]{2,1,0:T(8,128)(2,1)S(1)}, u32[]{:S(2)}, u32[]{:S(2)}) async-start(bf16[128,16,256]{2,1,0:T(8,128)(2,1)} %bitcast.6), calls=%async_computation | async-start | bytes 2097152 | tf_op jit(solution)/shard_map/all_to_all | solution.py:41
  17.8 19.2 %all-to-all-done = bf16[128,16,256]{2,1,0:T(8,128)(2,1)S(1)} async-done(((bf16[128,16,256]{2,1,0:T(8,128)(2,1)}), bf16[128,16,256]{2,1,0:T(8,128)(2,1)S(1)}, u32[]{:S(2)}, u32[]{:S(2)}) %all-to-all-start) | async-done | bytes 1048608 | tf_op jit(solution)/shard_map/all_to_all | solution.py:41
  37.0 0.9 select_reduce_fusion
  37.9 0.0 copy-start.4
  38.0 0.0 copy-start.5
  38.0 2.7 %fusion.132 = f32[2048,512]{1,0:T(8,128)} fusion(bf16[2048,256]{1,0:T(8,128)(2,1)S(1)} %bitcast.92, bf16[227,512]{1,0:T(8,128)(2,1)S(1)} %copy-done.7), kind=kOutput, calls=%fused_computation.147 | convolution fusion | flops 536870912 | bytes 5475328 | tf_op jit(solution)/shard_map/dot_general | solution.py:18
  40.6 3.0 %fusion.6 = f32[2048,512]{1,0:T(8,128)} fusion(bf16[256,512]{1,0:T(8,128)(2,1)S(1)} %copy-done.5, bf16[512,512]{1,0:T(8,128)(2,1)S(1)} %copy-done.4, f32[256]{0:T(256)S(1)} %iota_add_fusion, f32[2048]{0:T(1024)S(1)} %get-tuple-element.52), kind=kOutput, calls=%fused_computation.11 | convolution fusion | flops 671744000 | bytes 4989952 | tf_op jit(solution)/shard_map/dot_general | solution.py:18
  43.6 7.1 %multiply_add_fusion = f32[2048,512]{1,0:T(8,128)} fusion(f32[2048,512]{1,0:T(8,128)} %fusion.6, bf16[512,512]{1,0:T(8,128)(2,1)S(1)} %copy-done, f32[2048,512]{1,0:T(8,128)} %fusion.132, f32[512]{0:T(512)S(1)} %convert_element_type.165, f32[2048]{0:T(1024)S(1)} %get-tuple-element.51), kind=kOutput, calls=%fused_computation.3 | convolution fusion | flops 1082130432 | bytes 13117440 | tf_op jit(solution)/shard_map/dot_general | solution.py:18
  50.7 4.9 %add_convert_fusion.2 = (bf16[256,512]{1,0:T(8,128)(2,1)S(1)}, f32[256,512]{1,0:T(8,128)}) fusion(bf16[256,512]{1,0:T(8,128)(2,1)S(1)} %copy-done.5, bf16[512,512]{1,0:T(8,128)(2,1)S(1)} %copy-done.10, f32[2048,512]{1,0:T(8,128)} %multiply_add_fusion, f32[256]{0:T(256)S(1)} %iota_add_fusion, f32[2048]{0:T(1024)S(1)} %get-tuple-element.52), kind=kOutput, calls=%fused_computation.113 | convolution fusion | flops 677904384 | bytes 5776384 | tf_op jit(solution)/shard_map/dot_general | solution.py:18
  55.6 1.1 collective-permute-start
  56.6 1.3 fusion.96
  58.0 0.6 collective-permute-done
  58.6 2.7 %collective-permute-done.1 = bf16[128,512]{1,0:T(8,128)(2,1)S(1)} collective-permute-done((bf16[128,512]{1,0:T(8,128)(2,1)S(1)}, bf16[128,512]{1,0:T(8,128)(2,1)S(1)}, u32[]{:S(2)}, u32[]{:S(2)}) %collective-permute-start.1) | collective-permute-done | bytes 131104 | tf_op jit(solution)/shard_map/ppermute | solution.py:37
  61.3 4.1 %fusion.13 = f32[1536,512]{1,0:T(8,128)} fusion(s32[1536]{0:T(1024)S(1)} %eq.167, bf16[128,512]{1,0:T(8,128)(2,1)S(1)} %collective-permute-done.1, bf16[256,512]{1,0:T(8,128)(2,1)S(1)} %get-tuple-element.65, bf16[128,512]{1,0:T(8,128)(2,1)S(1)} %collective-permute-done, bf16[2,3,512,512]{3,2,1,0:T(8,128)(2,1)} %param.32), kind=kOutput, calls=%fused_computation.27 | convolution fusion | flops 1076363264 | bytes 4200448 | tf_op jit(solution)/shard_map/dot_general | solution.py:18
  65.4 2.9 %fusion.20 = f32[256,512]{1,0:T(8,128)S(1)} fusion(f32[6,256,512]{2,1,0:T(8,128)} %bitcast.87, f32[256,512]{1,0:T(8,128)S(1)} %fusion.96), kind=kLoop, calls=%fused_computation.34 | loop fusion | flops 4587520 | bytes 4194304 | tf_op jit(solution)/shard_map/reduce_sum | solution.py:102
  68.2 2.2 %add_convert_fusion.1 = (bf16[256,512]{1,0:T(8,128)(2,1)S(1)}, f32[256,512]{1,0:T(8,128)}) fusion(bf16[256,512]{1,0:T(8,128)(2,1)S(1)} %get-tuple-element.65, bf16[2,3,512,512]{3,2,1,0:T(8,128)(2,1)} %param.32, f32[256,512]{1,0:T(8,128)S(1)} %fusion.20), kind=kOutput, calls=%fused_computation.110 | convolution fusion | flops 135397376 | bytes 2097152 | tf_op jit(solution)/shard_map/dot_general | solution.py:18
  70.4 0.0 collective-permute-start.2
  70.5 0.8 collective-permute-start.3
  71.2 1.3 fusion.87
  72.6 0.0 collective-permute-done.2
  72.6 0.0 copy-start.11
  72.6 0.6 copy-done.11
  73.2 1.9 %collective-permute-done.3 = bf16[128,512]{1,0:T(8,128)(2,1)} collective-permute-done((bf16[128,512]{1,0:T(8,128)(2,1)S(1)}, bf16[128,512]{1,0:T(8,128)(2,1)}, u32[]{:S(2)}, u32[]{:S(2)}) %collective-permute-start.3) | collective-permute-done | bytes 131104 | tf_op jit(solution)/shard_map/ppermute | solution.py:37
  75.2 4.3 %fusion.12 = f32[1536,512]{1,0:T(8,128)} fusion(s32[1536]{0:T(1024)S(1)} %eq.167, bf16[128,512]{1,0:T(8,128)(2,1)} %collective-permute-done.3, bf16[256,512]{1,0:T(8,128)(2,1)S(1)} %get-tuple-element.67, bf16[128,512]{1,0:T(8,128)(2,1)} %copy-done.11, bf16[2,3,512,512]{3,2,1,0:T(8,128)(2,1)} %param.32), kind=kOutput, calls=%fused_computation.26 | convolution fusion | flops 1076363264 | bytes 4200448 | tf_op jit(solution)/shard_map/dot_general | solution.py:18
  79.4 3.0 %fusion.21 = f32[256,512]{1,0:T(8,128)S(1)} fusion(f32[6,256,512]{2,1,0:T(8,128)} %bitcast.89, f32[256,512]{1,0:T(8,128)S(1)} %fusion.87), kind=kLoop, calls=%fused_computation.35 | loop fusion | flops 4587520 | bytes 4194304 | tf_op jit(solution)/shard_map/reduce_sum | solution.py:102
  82.4 1.1 add_convert_fusion
  83.5 0.4 convolution_multiply_fusion.1
  83.9 0.5 copy-done.2
  84.4 1.5 fusion.30
  85.9 1.4 fusion.9
  87.3 1.3 fusion.177
  88.6 2.3 %collective-permute-start.5 = (bf16[128,512]{1,0:T(8,128)(2,1)S(1)}, bf16[128,512]{1,0:T(8,128)(2,1)S(1)}, u32[]{:S(2)}, u32[]{:S(2)}) collective-permute-start(bf16[128,512]{1,0:T(8,128)(2,1)S(1)} %get-tuple-element.55), channel_id=1, source_target_pairs={{0,7},{1,0},{2,1},{3,2},{4,3},{5,4},{6,5},{7,6},{8,15},{9,8},{10,9... | collective-permute-start | bytes 393224 | tf_op jit(solution)/shard_map/ppermute | solution.py:37
  90.9 0.3 convolution_add_fusion.4
  91.3 2.9 %collective-permute-done.4 = bf16[128,512]{1,0:T(8,128)(2,1)S(1)} collective-permute-done((bf16[128,512]{1,0:T(8,128)(2,1)S(1)}, bf16[128,512]{1,0:T(8,128)(2,1)S(1)}, u32[]{:S(2)}, u32[]{:S(2)}) %collective-permute-start.4) | collective-permute-done | bytes 131104 | tf_op jit(solution)/shard_map/ppermute | solution.py:37
  94.3 0.1 fusion.121
  94.3 0.3 convolution_add_fusion.3
  94.7 0.4 convolution_multiply_fusion
  95.1 1.1 copy-done.1
  96.1 1.3 fusion.31
  97.4 1.4 fusion.8
  98.8 1.3 fusion.178
  100.2 1.1 collective-permute-start.6
  101.3 0.3 convolution_add_fusion.2
  101.6 3.7 %collective-permute-start.7 = (bf16[128,512]{1,0:T(8,128)(2,1)S(1)}, bf16[128,512]{1,0:T(8,128)(2,1)S(1)}, u32[]{:S(2)}, u32[]{:S(2)}) collective-permute-start(bf16[128,512]{1,0:T(8,128)(2,1)S(1)} %get-tuple-element.53), channel_id=1, source_target_pairs={{0,7},{1,0},{2,1},{3,2},{4,3},{5,4},{6,5},{7,6},{8,15},{9,8},{10,9... | collective-permute-start | bytes 393224 | tf_op jit(solution)/shard_map/ppermute | solution.py:37
  105.3 0.4 collective-permute-done.6
  105.8 0.5 collective-permute-done.7
  106.3 0.1 fusion.119
  106.4 0.3 convolution_add_fusion.1
  106.7 5.1 %multiply_convert_fusion.1 = bf16[2048,512]{1,0:T(8,128)(2,1)} fusion(f32[2048,512]{1,0:T(8,128)} %multiply_add_fusion, bf16[512,512]{1,0:T(8,128)(2,1)S(1)} %copy-done.10, f32[256]{0:T(256)S(1)} %iota_add_fusion, f32[2048]{0:T(1024)S(1)} %get-tuple-element.52, f32[256,512]{1,0:T(8,128)S(1)} %convolution_add_fusion.1, f32[256,512]{1,0:T(8,128)S(1)} %copy-done.13), kind=kOutput, calls=%fused_computation.1 | convolution fusion | flops 682360832 | bytes 7873536 | tf_op jit(solution)/shard_map/dot_general | solution.py:18
  111.8 6.0 %convolution_convert_fusion = bf16[2048,256]{1,0:T(8,128)(2,1)} fusion(bf16[2048,512]{1,0:T(8,128)(2,1)} %multiply_convert_fusion.1, bf16[512,512]{1,0:T(8,128)(2,1)S(1)} %copy-done, f32[2048,512]{1,0:T(8,128)} %fusion.132, bf16[227,512]{1,0:T(8,128)(2,1)S(1)} %copy-done.7), kind=kOutput, calls=%fused_computation.36 | convolution fusion | flops 1620574208 | bytes 8096768 | tf_op jit(solution)/shard_map/dot_general | solution.py:22
  117.8 9.0 %all-to-all-start.1 = ((bf16[128,16,256]{2,1,0:T(8,128)(2,1)}), bf16[128,16,256]{2,1,0:T(8,128)(2,1)S(1)}, u32[]{:S(2)}, u32[]{:S(2)}) async-start(bf16[128,16,256]{2,1,0:T(8,128)(2,1)} %bitcast.21), calls=%async_computation.1 | async-start | bytes 2097152 | tf_op jit(solution)/shard_map/all_to_all | solution.py:41
  126.9 3.6 %fusion.32 = bf16[256,512]{1,0:T(8,128)(2,1)} fusion(f32[256,512]{1,0:T(8,128)S(1)} %convolution_add_fusion.1, bf16[512,512]{1,0:T(8,128)(2,1)S(1)} %copy-done.4, bf16[2048,512]{1,0:T(8,128)(2,1)} %multiply_convert_fusion.1, f32[256]{0:T(256)S(1)} %iota_add_fusion, f32[2048]{0:T(1024)S(1)} %get-tuple-element.52), kind=kOutput, calls=%fused_computation.57 | convolution fusion | flops 672006144 | bytes 3417088 | tf_op jit(solution)/shard_map/dot_general | solution.py:22
  130.5 15.7 %all-to-all-done.1 = bf16[128,16,256]{2,1,0:T(8,128)(2,1)S(1)} async-done(((bf16[128,16,256]{2,1,0:T(8,128)(2,1)}), bf16[128,16,256]{2,1,0:T(8,128)(2,1)S(1)}, u32[]{:S(2)}, u32[]{:S(2)}) %all-to-all-start.1) | async-done | bytes 1048608 | tf_op jit(solution)/shard_map/all_to_all | solution.py:41
  146.2 0.7 fusion.41
  146.9 0.7 slice.281
  (37 shorter events, 0.3 us)
Async XLA Ops:
  0.6 43.0 %copy-start = (bf16[512,512]{1,0:T(8,128)(2,1)S(1)}, bf16[512,512]{1,0:T(8,128)(2,1)}, u32[]{:S(2)}) copy-start(bf16[512,512]{1,0:T(8,128)(2,1)} %param.28) | copy-start | bytes 1572868
  0.6 17.1 %copy-start.9 = (bf16[512]{0:T(512)(128)(2,1)S(1)}, bf16[512]{0:T(512)(128)(2,1)}, u32[]{:S(2)}) copy-start(bf16[512]{0:T(512)(128)(2,1)} %param.31) | copy-start | bytes 3076
  0.7 17.1 %copy-start.8 = (s32[256,6]{0,1:T(8,128)S(1)}, s32[256,6]{0,1:T(8,128)}, u32[]{:S(2)}) copy-start(s32[256,6]{0,1:T(8,128)} %param.26) | copy-start | bytes 18436
  2.5 35.4 %copy-start.7 = (bf16[227,512]{1,0:T(8,128)(2,1)S(1)}, bf16[227,512]{1,0:T(8,128)(2,1)}, u32[]{:S(2)}) copy-start(bf16[227,512]{1,0:T(8,128)(2,1)} %param.27) | copy-start | bytes 697348
  6.2 30.8 %all-to-all-start = ((bf16[128,16,256]{2,1,0:T(8,128)(2,1)}), bf16[128,16,256]{2,1,0:T(8,128)(2,1)S(1)}, u32[]{:S(2)}, u32[]{:S(2)}) async-start(bf16[128,16,256]{2,1,0:T(8,128)(2,1)} %bitcast.6), calls=%async_computation | async-start | bytes 2097152 | tf_op jit(solution)/shard_map/all_to_all | solution.py:41
  37.9 2.7 %copy-start.4 = (bf16[512,512]{1,0:T(8,128)(2,1)S(1)}, bf16[512,512]{1,0:T(8,128)(2,1)}, u32[]{:S(2)}) copy-start(bf16[512,512]{1,0:T(8,128)(2,1)} %param.29) | copy-start | bytes 1572868
  38.0 2.7 %copy-start.5 = (bf16[256,512]{1,0:T(8,128)(2,1)S(1)}, bf16[256,512]{1,0:T(8,128)(2,1)}, u32[]{:S(2)}) copy-start(bf16[256,512]{1,0:T(8,128)(2,1)} %param.22) | copy-start | bytes 786436
  43.6 7.1 %copy-start.10 = (bf16[512,512]{1,0:T(8,128)(2,1)S(1)}, bf16[512,512]{1,0:T(8,128)(2,1)}, u32[]{:S(2)}) copy-start(bf16[512,512]{1,0:T(8,128)(2,1)} %param.30) | copy-start | bytes 1572868
  55.6 3.0 %collective-permute-start = (bf16[128,512]{1,0:T(8,128)(2,1)S(1)}, bf16[128,512]{1,0:T(8,128)(2,1)S(1)}, u32[]{:S(2)}, u32[]{:S(2)}) collective-permute-start(bf16[128,512]{1,0:T(8,128)(2,1)S(1)} %get-tuple-element.59), channel_id=1, source_target_pairs={{0,1},{1,2},{2,3},{3,4},{4,5},{5,6},{6,7},{7,0},{8,9},{9,10},{10,1... | collective-permute-start | bytes 393224 | tf_op jit(solution)/shard_map/ppermute | solution.py:37
  56.6 4.7 %collective-permute-start.1 = (bf16[128,512]{1,0:T(8,128)(2,1)S(1)}, bf16[128,512]{1,0:T(8,128)(2,1)S(1)}, u32[]{:S(2)}, u32[]{:S(2)}) collective-permute-start(bf16[128,512]{1,0:T(8,128)(2,1)S(1)} %get-tuple-element.60), channel_id=1, source_target_pairs={{0,7},{1,0},{2,1},{3,2},{4,3},{5,4},{6,5},{7,6},{8,15},{9,8},{10,9... | collective-permute-start | bytes 393224 | tf_op jit(solution)/shard_map/ppermute | solution.py:37
  70.4 2.1 %collective-permute-start.2 = (bf16[128,512]{1,0:T(8,128)(2,1)S(1)}, bf16[128,512]{1,0:T(8,128)(2,1)S(1)}, u32[]{:S(2)}, u32[]{:S(2)}) collective-permute-start(bf16[128,512]{1,0:T(8,128)(2,1)S(1)} %get-tuple-element.57), channel_id=1, source_target_pairs={{0,1},{1,2},{2,3},{3,4},{4,5},{5,6},{6,7},{7,0},{8,9},{9,10},{10,1... | collective-permute-start | bytes 393224 | tf_op jit(solution)/shard_map/ppermute | solution.py:37
  70.5 4.7 %collective-permute-start.3 = (bf16[128,512]{1,0:T(8,128)(2,1)S(1)}, bf16[128,512]{1,0:T(8,128)(2,1)}, u32[]{:S(2)}, u32[]{:S(2)}) collective-permute-start(bf16[128,512]{1,0:T(8,128)(2,1)S(1)} %get-tuple-element.58), channel_id=1, source_target_pairs={{0,7},{1,0},{2,1},{3,2},{4,3},{5,4},{6,5},{7,6},{8,15},{9,8},{10,9... | collective-permute-start | bytes 393224 | tf_op jit(solution)/shard_map/ppermute | solution.py:37
  72.6 0.7 copy-start.11
  79.4 3.0 %copy-start.3 = (bf16[2,3,512,512]{3,2,1,0:T(8,128)(2,1)S(1)}, bf16[2,3,512,512]{3,2,1,0:T(8,128)(2,1)}, u32[]{:S(2)}) copy-start(bf16[2,3,512,512]{3,2,1,0:T(8,128)(2,1)} %param.32) | copy-start | bytes 9437188
  79.4 4.1 %copy-start.6 = (bf16[256,512]{1,0:T(8,128)(2,1)S(1)}, bf16[256,512]{1,0:T(8,128)(2,1)}, u32[]{:S(2)}) copy-start(bf16[256,512]{1,0:T(8,128)(2,1)} %param.33) | copy-start | bytes 786436
  82.4 2.0 %copy-start.2 = (f32[1536,512]{1,0:T(8,128)S(1)}, f32[1536,512]{1,0:T(8,128)}, u32[]{:S(2)}) copy-start(f32[1536,512]{1,0:T(8,128)} %fusion.12) | copy-start | bytes 9437188
  88.6 6.0 %copy-start.12 = (f32[256,512]{1,0:T(8,128)S(1)}, f32[256,512]{1,0:T(8,128)}, u32[]{:S(2)}) copy-start(f32[256,512]{1,0:T(8,128)} %get-tuple-element.68) | copy-start | bytes 1572868
  88.6 5.6 %collective-permute-start.5 = (bf16[128,512]{1,0:T(8,128)(2,1)S(1)}, bf16[128,512]{1,0:T(8,128)(2,1)S(1)}, u32[]{:S(2)}, u32[]{:S(2)}) collective-permute-start(bf16[128,512]{1,0:T(8,128)(2,1)S(1)} %get-tuple-element.55), channel_id=1, source_target_pairs={{0,7},{1,0},{2,1},{3,2},{4,3},{5,4},{6,5},{7,6},{8,15},{9,8},{10,9... | collective-permute-start | bytes 393224 | tf_op jit(solution)/shard_map/ppermute | solution.py:37
  90.9 3.3 %collective-permute-start.4 = (bf16[128,512]{1,0:T(8,128)(2,1)S(1)}, bf16[128,512]{1,0:T(8,128)(2,1)S(1)}, u32[]{:S(2)}, u32[]{:S(2)}) collective-permute-start(bf16[128,512]{1,0:T(8,128)(2,1)S(1)} %get-tuple-element.56), channel_id=1, source_target_pairs={{0,1},{1,2},{2,3},{3,4},{4,5},{5,6},{6,7},{7,0},{8,9},{9,10},{10,1... | collective-permute-start | bytes 393224 | tf_op jit(solution)/shard_map/ppermute | solution.py:37
  94.2 1.9 %copy-start.1 = (f32[1536,512]{1,0:T(8,128)S(1)}, f32[1536,512]{1,0:T(8,128)}, u32[]{:S(2)}) copy-start(f32[1536,512]{1,0:T(8,128)} %fusion.13) | copy-start | bytes 9437188
  100.2 6.6 %copy-start.13 = (f32[256,512]{1,0:T(8,128)S(1)}, f32[256,512]{1,0:T(8,128)}, u32[]{:S(2)}) copy-start(f32[256,512]{1,0:T(8,128)} %get-tuple-element.66) | copy-start | bytes 1572868
  100.2 5.6 %collective-permute-start.6 = (bf16[128,512]{1,0:T(8,128)(2,1)S(1)}, bf16[128,512]{1,0:T(8,128)(2,1)S(1)}, u32[]{:S(2)}, u32[]{:S(2)}) collective-permute-start(bf16[128,512]{1,0:T(8,128)(2,1)S(1)} %get-tuple-element.54), channel_id=1, source_target_pairs={{0,1},{1,2},{2,3},{3,4},{4,5},{5,6},{6,7},{7,0},{8,9},{9,10},{10,1... | collective-permute-start | bytes 393224 | tf_op jit(solution)/shard_map/ppermute | solution.py:37
  101.6 4.6 %collective-permute-start.7 = (bf16[128,512]{1,0:T(8,128)(2,1)S(1)}, bf16[128,512]{1,0:T(8,128)(2,1)S(1)}, u32[]{:S(2)}, u32[]{:S(2)}) collective-permute-start(bf16[128,512]{1,0:T(8,128)(2,1)S(1)} %get-tuple-element.53), channel_id=1, source_target_pairs={{0,7},{1,0},{2,1},{3,2},{4,3},{5,4},{6,5},{7,6},{8,15},{9,8},{10,9... | collective-permute-start | bytes 393224 | tf_op jit(solution)/shard_map/ppermute | solution.py:37
  117.8 28.4 %all-to-all-start.1 = ((bf16[128,16,256]{2,1,0:T(8,128)(2,1)}), bf16[128,16,256]{2,1,0:T(8,128)(2,1)S(1)}, u32[]{:S(2)}, u32[]{:S(2)}) async-start(bf16[128,16,256]{2,1,0:T(8,128)(2,1)} %bitcast.21), calls=%async_computation.1 | async-start | bytes 2097152 | tf_op jit(solution)/shard_map/all_to_all | solution.py:41
where the time goes:
time: 148 us
  matrix products  53.7 us (36%)
  waiting for transfers between devices  44 us (30%)
  starting transfers between devices  29.4 us (20%)
  other arithmetic  13.5 us (9%)
  local copies, waits for them, and re-layouts  5.82 us (4%)
    dot_general x13, matrix products, mm(): lax.dot_general(left, right, (((1,), (0,)), ((), ())), preferred_element_...  38.6 us
    all_to_all x2, waiting for transfers between devices, exchange(): return lax.all_to_all(x, AXES, split_axis=0, concat_axis=0, tiled=True)  35 us
    all_to_all x2, starting transfers between devices, exchange(): return lax.all_to_all(x, AXES, split_axis=0, concat_axis=0, tiled=True)  20.5 us
    dot_general x8, matrix products, mm_t(): lax.dot_general(left, right, (((1,), (1,)), ((), ())), preferred_element_...  11.7 us
    ppermute x8, waiting for transfers between devices, shift(): lax.ppermute(x, 'patch', [(i, (i + (1 if up else -1)) % n) for i in range...  9.07 us
    ppermute x8, starting transfers between devices, shift(): lax.ppermute(x, 'patch', [(i, (i + (1 if up else -1)) % n) for i in range...  8.94 us
    reduce_sum x2, other arithmetic, local(): mean_msg = (proc.sum(axis=0) / DEG).astype(BF16)  5.86 us
    dot_general x3, matrix products, t_mm(): lax.dot_general(left, right, (((0,), (0,)), ((), ())), preferred_element_...  3.34 us
  transfers between devices with their start and end apart: 10, of which 8 were waited for; matrix products, arithmetic and copies ran while one was open for 5% of the time, Pallas kernels for 0%

commit v1 on v0

v1 whole, which is shorter than its diff:
```python
import functools

import jax
import jax.numpy as jnp
from jax import lax
from jax.experimental import pallas as pl
from jax.experimental.pallas import tpu as pltpu
from jax.sharding import PartitionSpec as P

TOP = 4
DEG = 6
RIM = 128
LAYERS = 2
CAP = 16
WIDE = 256
META = 240
AXES = ("band", "patch")
F32 = jnp.float32
BF16 = jnp.bfloat16
I32 = jnp.int32
GROUP = 16
ROWS = GROUP * CAP


def mm(left, right):
    return lax.dot_general(left, right, (((1,), (0,)), ((), ())), preferred_element_type=F32)


def mm_t(left, right):
    return lax.dot_general(left, right, (((1,), (1,)), ((), ())), preferred_element_type=F32)


def act(value):
    sig = 0.5 * jnp.tanh(0.5 * value) + 0.5
    out = value * sig
    return out, sig + out * (1.0 - sig)


def iota(shape, dim):
    return lax.broadcasted_iota(I32, shape, dim)


def onehot(mask):
    return jnp.where(mask, 1.0, 0.0).astype(BF16)


def offsets(slot):
    dp = slot % 8
    return (slot // 8 + 5 * dp) % 16, dp


def kernel(
    feat_t, dest_t, node_t, dist_t, src_t, w_embed, edge_vec,
    state_hbm, w_send_hbm, w_recv_hbm, w_node_hbm, proc_hbm, cot_hbm,
    mesh_out, mesh_grad, grid_grad_t,
    state, w_send, w_recv, w_node, proc, cot, w_emb,
    w_send_t, w_recv_t, w_node_t, proc_t, w_emb_t,
    meta, packed_t, packed, place, send_buf, recv_buf, back_buf, ret_buf, unpick,
    recv_proj, here, here_t, d_emb, d_enc, acc, d_node,
    chosen, chosen_t, pre, d_proc, d_upd, hid, send_p, grad_pre, grad_ext, grad, rims,
    load_sem, fwd_send, fwd_recv, bwd_send, bwd_recv, rim_send, rim_recv, entered,
):
    bands, patches = lax.axis_size("band"), lax.axis_size("patch")
    peers = bands * patches
    groups = peers // GROUP
    nodes, width = state.shape
    cin, rows = feat_t.shape
    b, p = lax.axis_index("band"), lax.axis_index("patch")
    left, right = (p + patches - 1) % patches, (p + 1) % patches

    loads = [
        pltpu.make_async_copy(src, dst, load_sem.at[i])
        for i, (src, dst) in enumerate(
            [(state_hbm, state), (w_recv_hbm, w_recv), (w_send_hbm, w_send), (w_node_hbm, w_node), (proc_hbm, proc), (cot_hbm, cot)]
        )
    ]
    for load in loads:
        load.start()

    barrier = pltpu.get_barrier_semaphore()

    def greet_patch(i, carry):
        pl.semaphore_signal(barrier, inc=1, device_id=(b, (p + i) % patches), device_id_type=pl.DeviceIdType.MESH)
        return carry

    def greet_band(i, carry):
        pl.semaphore_signal(barrier, inc=1, device_id=((b + i) % bands, p), device_id_type=pl.DeviceIdType.MESH)
        return carry

    lax.fori_loop(1, patches, greet_patch, 0)
    lax.fori_loop(1, bands, greet_band, 0)

    meta[...] = jnp.zeros_like(meta)
    dest = dest_t[...]
    meta[0:TOP, :] = (dest + 1).astype(F32)
    meta[TOP : 2 * TOP, :] = (node_t[...] + 1).astype(F32)
    meta[2 * TOP : 3 * TOP, :] = dist_t[...].astype(F32)
    packed_t[...] = jnp.zeros_like(packed_t)
    packed_t[0:cin, :] = feat_t[...]
    packed_t[META:WIDE, :] = meta[...].astype(BF16)
    packed[...] = packed_t[...].T
    slot = iota((peers, rows), 0)
    slot_p = slot & (patches - 1)
    slot_b = (lax.shift_right_logical(slot, 3) + 5 * slot_p) & (bands - 1)
    slot_id = ((slot_b + b) & (bands - 1)) * patches + ((slot_p + p) & (patches - 1))
    named = jnp.zeros((peers, rows), F32)
    for k in range(TOP):
        named = named + jnp.where(dest[k : k + 1, :] == slot_id, 1.0, 0.0)
    before = onehot(iota((rows, rows), 0) < iota((rows, rows), 1))
    rank = mm(named.astype(BF16), before)
    place[...] = jnp.where(named > 0.5, rank, -1.0).astype(BF16)

    def pick_group(g):
        spread = onehot(lax.shift_right_logical(iota((ROWS, peers), 0) + g * ROWS, 4) == iota((ROWS, peers), 1))
        slot_place = mm(spread, place[...])
        return onehot(slot_place == (iota((ROWS, rows), 0) & (CAP - 1)).astype(F32))

    def fill(g, carry):
        send_buf[pl.ds(pl.multiple_of(g * ROWS, ROWS), ROWS), :] = mm(pick_group(g), packed[...]).astype(BF16)
        return carry

    lax.fori_loop(0, groups, fill, 0)

    pl.semaphore_wait(barrier, patches + bands - 2)

    def greet_again(i, carry):
        pl.semaphore_signal(entered, inc=1, device_id=((b + i) % bands, p), device_id_type=pl.DeviceIdType.MESH)
        return carry

    lax.fori_loop(1, bands, greet_again, 0)
    pl.semaphore_wait(entered, bands - 1)

    def block(t):
        return pl.ds(pl.multiple_of(t * CAP, CAP), CAP)

    def send_fwd(t, carry):
        db, dp = offsets(t)
        pltpu.make_async_remote_copy(
            send_buf.at[block(t), :], recv_buf.at[block(t), :], fwd_send, fwd_recv.at[t // GROUP],
            device_id=((b + db) % bands, (p + dp) % patches), device_id_type=pl.DeviceIdType.MESH,
        ).start()
        return carry

    def send_bwd(t, carry):
        db, dp = offsets(t)
        pltpu.make_async_remote_copy(
            back_buf.at[block(t), :], ret_buf.at[block(t), :], bwd_send, bwd_recv.at[t // GROUP],
            device_id=((b + bands - db) % bands, (p + patches - dp) % patches), device_id_type=pl.DeviceIdType.MESH,
        ).start()
        return carry

    pltpu.make_async_copy(send_buf.at[pl.ds(0, CAP), :], recv_buf.at[pl.ds(0, CAP), :], fwd_recv.at[0]).start()
    lax.fori_loop(1, peers, send_fwd, 0)

    w_emb[...] = jnp.zeros_like(w_emb)
    w_emb[0:cin, :] = w_embed[...]
    w_emb_t[...] = w_emb[...].T
    loads[0].wait()
    loads[1].wait()
    recv_proj[...] = mm(state[...], w_recv[...]).astype(BF16)
    w_recv_t[...] = w_recv[...].T
    loads[2].wait()
    w_send_t[...] = w_send[...].T
    loads[3].wait()
    w_node_t[...] = w_node[...].T
    loads[4].wait()
    for layer in range(LAYERS):
        for i in range(3):
            proc_t[layer, i] = proc[layer, i].T
    loads[5].wait()
    unit = onehot(iota((ROWS, ROWS), 0) == iota((ROWS, ROWS), 1))
    src = src_t[...]
    here_first = (b * patches + p) * nodes
    left_first = (b * patches + left) * nodes
    right_first = (b * patches + right) * nodes
    for k in range(DEG):
        row = src[k : k + 1, :]
        own_row = jnp.where((row >= here_first) & (row < here_first + nodes), row - here_first, -1)
        rim_row = jnp.where(
            (row >= left_first + nodes - RIM) & (row < left_first + nodes),
            row - left_first - (nodes - RIM),
            jnp.where((row >= right_first) & (row < right_first + RIM), row - right_first + RIM, -1),
        )
        e = iota((nodes, nodes), 0)
        own_t = onehot(own_row == e)
        rim_t = onehot(rim_row == e)
        cols = slice(k * nodes, (k + 1) * nodes)
        chosen_t[0:nodes, cols] = own_t
        chosen_t[nodes : 2 * nodes, cols] = rim_t
        chosen[cols, 0:nodes] = mm_t(unit, own_t).astype(BF16)
        chosen[cols, nodes : 2 * nodes] = mm_t(unit, rim_t).astype(BF16)

    def fill_unpick(g, carry):
        unpick[g] = mm_t(unit, pick_group(g)).astype(BF16)
        return carry

    lax.fori_loop(0, groups, fill_unpick, 0)

    me1 = (b * patches + p + 1).astype(F32)
    c0 = META - 128
    sel_c, sel_l = iota((128, 384), 0), iota((128, 384), 1)
    sel_k = sel_l & 127
    select = onehot((sel_k < TOP) & (sel_c == c0 + sel_k + TOP * lax.shift_right_logical(sel_l, 7)))
    select_t = onehot(iota((16, 128), 1) == c0 + iota((16, 128), 0))
    ones = jnp.ones((128, nodes), BF16)
    edges = jnp.broadcast_to(edge_vec[...].astype(F32), (128, width)).astype(BF16)
    acc[...] = jnp.zeros_like(acc)

    def encode(g, carry):
        at = pl.ds(pl.multiple_of(g * ROWS, ROWS), ROWS)
        pltpu.make_async_copy(recv_buf.at[at, :], recv_buf.at[at, :], fwd_recv.at[g]).wait()
        got = recv_buf[at, :]
        tail = got[:, 128:256]
        fields = mm(tail, select)
        mine = fields[:, 0:128] == me1
        node = mm(jnp.where(mine, fields[:, 128:256], 0.0).astype(BF16), ones)
        length = mm(jnp.where(mine, fields[:, 256:384], 0.0).astype(BF16), edges)
        at_node = onehot(node == (iota((ROWS, nodes), 1) + 1).astype(F32))
        here[at, :] = at_node
        fields_t = mm_t(select_t, tail)
        node_row = jnp.zeros((1, ROWS), F32)
        for k in range(TOP):
            node_row = node_row + jnp.where(fields_t[k : k + 1, :] == me1, fields_t[TOP + k : TOP + k + 1, :], 0.0)
        at_node_t = onehot(node_row == (iota((nodes, ROWS), 0) + 1).astype(F32))
        here_t[g] = at_node_t
        latent, slope = act(mm(got, w_emb[...]))
        d_emb[at, :] = slope.astype(BF16)
        enc, slope = act(mm(latent.astype(BF16), w_send[...]) + mm(at_node, recv_proj[...]) + length)
        d_enc[at, :] = slope.astype(BF16)
        acc[...] += mm(at_node_t, enc.astype(BF16))
        return carry

    lax.fori_loop(0, groups, encode, 0)

    upd, slope = act(mm(acc[...].astype(BF16), w_node[...]))
    d_node[...] = slope
    hid[0] = (state[...].astype(F32) + upd).astype(BF16)

    def swap_rims(step, to_left, to_right):
        one = pltpu.make_async_remote_copy(
            to_left, rims.at[step, 1], rim_send.at[step, 0], rim_recv.at[step, 1],
            device_id=(b, left), device_id_type=pl.DeviceIdType.MESH,
        )
        two = pltpu.make_async_remote_copy(
            to_right, rims.at[step, 0], rim_send.at[step, 1], rim_recv.at[step, 0],
            device_id=(b, right), device_id_type=pl.DeviceIdType.MESH,
        )
        one.start()
        two.start()
        return one, two

    swaps = []
    for layer in range(LAYERS):
        one, two = swap_rims(layer, hid.at[layer, pl.ds(0, RIM), :], hid.at[layer, pl.ds(nodes - RIM, RIM), :])
        swaps += [one, two]
        now = hid[layer]
        recv_p = mm(now, proc[layer, 1])
        send_p[0:nodes, :] = mm(now, proc[layer, 0]).astype(BF16)
        one.wait_recv()
        two.wait_recv()
        send_p[nodes : nodes + RIM, :] = mm(rims[layer, 0], proc[layer, 0]).astype(BF16)
        send_p[nodes + RIM : nodes + 2 * RIM, :] = mm(rims[layer, 1], proc[layer, 0]).astype(BF16)
        for k in range(DEG):
            at = slice(k * nodes, (k + 1) * nodes)
            out, slope = act(recv_p + mm(chosen[at, :], send_p[...]))
            d_proc[layer, at, :] = slope.astype(BF16)
            acc[...] = out if k == 0 else acc[...] + out
        upd, slope = act(mm((acc[...] * (1.0 / DEG)).astype(BF16), proc[layer, 2]))
        d_upd[layer] = slope
        after = (now.astype(F32) + upd).astype(BF16)
        if layer + 1 < LAYERS:
            hid[layer + 1] = after
        else:
            mesh_out[...] = after

    grad[...] = cot[...].astype(F32)
    for layer in reversed(range(LAYERS)):
        mean = mm((grad[...] * d_upd[layer]).astype(BF16), proc_t[layer, 2]) * (1.0 / DEG)
        for k in range(DEG):
            at = slice(k * nodes, (k + 1) * nodes)
            part = mean * d_proc[layer, at, :].astype(F32)
            grad_pre[at, :] = part.astype(BF16)
            acc[...] = part if k == 0 else acc[...] + part
        grad_ext[layer] = mm(chosen_t[nodes : 2 * nodes, :], grad_pre[...]).astype(BF16)
        one, two = swap_rims(LAYERS + layer, grad_ext.at[layer, pl.ds(0, RIM), :], grad_ext.at[layer, pl.ds(RIM, RIM), :])
        swaps += [one, two]
        own = mm(chosen_t[0:nodes, :], grad_pre[...])
        grad[...] += mm(acc[...].astype(BF16), proc_t[layer, 1])
        one.wait_recv()
        two.wait_recv()
        rim = jnp.concatenate([rims[LAYERS + layer, 0], rims[LAYERS + layer, 1]], axis=0)
        grad[...] += mm((own + rim.astype(F32)).astype(BF16), proc_t[layer, 0])

    agg = mm((grad[...] * d_node[...]).astype(BF16), w_node_t[...]).astype(BF16)
    recv_proj[...] = agg

    def decode(g, carry):
        at = pl.ds(pl.multiple_of(g * ROWS, ROWS), ROWS)
        edge = (mm(here[at, :], recv_proj[...]) * d_enc[at, :].astype(F32)).astype(BF16)
        d_enc[at, :] = edge
        emb = (mm(edge, w_send_t[...]) * d_emb[at, :].astype(F32)).astype(BF16)
        back_buf[at, :] = mm(emb, w_emb_t[...]).astype(BF16)
        lax.fori_loop(jnp.maximum(g * GROUP, 1), (g + 1) * GROUP, send_bwd, 0)
        return carry

    lax.fori_loop(0, groups, decode, 0)
    pltpu.make_async_copy(back_buf.at[pl.ds(0, CAP), :], ret_buf.at[pl.ds(0, CAP), :], bwd_recv.at[0]).start()
    acc[...] = jnp.zeros_like(acc)

    def scatter(g, carry):
        at = pl.ds(pl.multiple_of(g * ROWS, ROWS), ROWS)
        acc[...] += mm(here_t[g], d_enc[at, :])
        return carry

    lax.fori_loop(0, groups, scatter, 0)
    mesh_grad[...] = (grad[...] + mm(acc[...].astype(BF16), w_recv_t[...])).astype(BF16)

    acc[...] = jnp.zeros_like(acc)

    def collect(g, carry):
        at = pl.ds(pl.multiple_of(g * ROWS, ROWS), ROWS)
        pltpu.make_async_copy(ret_buf.at[at, :], ret_buf.at[at, :], bwd_recv.at[g]).wait()
        acc[:, 0:WIDE] += mm(unpick[g], ret_buf[at, :])
        return carry

    lax.fori_loop(0, groups, collect, 0)
    packed_t[...] = mm_t(unit, acc[:, 0:WIDE].astype(BF16)).astype(BF16)
    grid_grad_t[...] = packed_t[0:cin, :]

    for swap in swaps:
        swap.wait_send()
    others = pl.ds(CAP, (peers - 1) * CAP)
    pltpu.make_async_copy(send_buf.at[others, :], send_buf.at[others, :], fwd_send).wait()
    pltpu.make_async_copy(back_buf.at[others, :], back_buf.at[others, :], bwd_send).wait()


def local(grid_feat, mesh_state, g2m_dest, g2m_node, g2m_dist, mesh_src, w_embed, w_send, w_recv, w_node, edge_vec, proc_weights, cotangent):
    peers = lax.axis_size(AXES)
    rows, cin = grid_feat.shape
    nodes, width = mesh_state.shape
    slots = peers * CAP
    groups = peers // GROUP
    vmem = pl.BlockSpec(memory_space=pltpu.VMEM)
    anywhere = pl.BlockSpec(memory_space=pl.ANY)
    square = pltpu.VMEM((width, width), BF16)
    stack = pltpu.VMEM((LAYERS, 3, width, width), BF16)
    tile = pltpu.VMEM((nodes, width), BF16)
    mesh_out, mesh_grad, grid_grad_t = pl.pallas_call(
        kernel,
        out_shape=(
            jax.ShapeDtypeStruct((nodes, width), BF16),
            jax.ShapeDtypeStruct((nodes, width), BF16),
            jax.ShapeDtypeStruct((cin, rows), BF16),
        ),
        in_specs=[vmem] * 7 + [anywhere] * 6,
        out_specs=(vmem,) * 3,
        scratch_shapes=[
            tile, square, square, square, stack, tile, pltpu.VMEM((WIDE, width), BF16),
            square, square, square, stack, pltpu.VMEM((width, WIDE), BF16),
            pltpu.VMEM((16, rows), F32), pltpu.VMEM((WIDE, rows), BF16), pltpu.VMEM((rows, WIDE), BF16),
            pltpu.VMEM((peers, rows), BF16),
            pltpu.VMEM((slots, WIDE), BF16), pltpu.VMEM((slots, WIDE), BF16),
            pltpu.VMEM((slots, WIDE), BF16), pltpu.VMEM((slots, WIDE), BF16),
            pltpu.VMEM((groups, rows, ROWS), BF16),
            tile, pltpu.VMEM((slots, nodes), BF16), pltpu.VMEM((groups, nodes, ROWS), BF16),
            pltpu.VMEM((slots, width), BF16), pltpu.VMEM((slots, width), BF16),
            pltpu.VMEM((nodes, width), F32), pltpu.VMEM((nodes, width), F32),
            pltpu.VMEM((DEG * nodes, 2 * nodes), BF16), pltpu.VMEM((2 * nodes, DEG * nodes), BF16),
            pltpu.VMEM((DEG * nodes, width), F32),
            pltpu.VMEM((LAYERS, DEG * nodes, width), BF16), pltpu.VMEM((LAYERS, nodes, width), F32),
            pltpu.VMEM((LAYERS, nodes, width), BF16), pltpu.VMEM((2 * nodes, width), BF16),
            pltpu.VMEM((DEG * nodes, width), BF16), pltpu.VMEM((LAYERS, 2 * RIM, width), BF16),
            pltpu.VMEM((nodes, width), F32), pltpu.VMEM((2 * LAYERS, 2, RIM, width), BF16),
            pltpu.SemaphoreType.DMA((6,)),
            pltpu.SemaphoreType.DMA, pltpu.SemaphoreType.DMA((groups,)),
            pltpu.SemaphoreType.DMA, pltpu.SemaphoreType.DMA((groups,)),
            pltpu.SemaphoreType.DMA((2 * LAYERS, 2)), pltpu.SemaphoreType.DMA((2 * LAYERS, 2)),
            pltpu.SemaphoreType.REGULAR,
        ],
        compiler_params=pltpu.CompilerParams(
            collective_id=0, has_side_effects=True, vmem_limit_bytes=56 * 2**20
        ),
    )(
        grid_feat.T, g2m_dest.T, g2m_node.T, g2m_dist.T, mesh_src.T, w_embed, edge_vec.reshape(1, width),
        mesh_state, w_send, w_recv, w_node, proc_weights, cotangent,
    )
    return mesh_out, mesh_grad, grid_grad_t.T


def solution(mesh):
    split = P(AXES, None)
    return jax.shard_map(
        local,
        mesh=mesh,
        in_specs=(split,) * 6 + (P(),) * 6 + (split,),
        out_specs=(split,) * 3,
        check_vma=False,
    )
```

time: 148 us -> 78.2 us (0.53)
  Pallas kernels: 0 us -> 71.2 us
  matrix products: 53.7 us -> 0 us
  waiting for transfers between devices: 44 us -> 0 us
  starting transfers between devices: 29.4 us -> 0 us
  other arithmetic: 13.5 us -> 0 us
    pallas_call x0 -> x1, Pallas kernels: none -> 71.2 us  [local(): pl.pallas_call(kernel, out_shape=(jax.ShapeDtypeStruct((nodes, width), BF...]
    dot_general x24 -> x0, matrix products: 53.7 us -> none  [the longest x13 38.6 us: mm(): lax.dot_general(left, right, (((1,), (0,)), ((), ())), preferred_element_...]
    all_to_all x2 -> x0, waiting for transfers between devices: 35 us -> none  [exchange(): return lax.all_to_all(x, AXES, split_axis=0, concat_axis=0, tiled=True)]
    all_to_all x2 -> x0, starting transfers between devices: 20.5 us -> none  [exchange(): return lax.all_to_all(x, AXES, split_axis=0, concat_axis=0, tiled=True)]
    reduce_sum x5 -> x0, other arithmetic: 9.48 us -> none  [the longest x2 5.86 us: local(): mean_msg = (proc.sum(axis=0) / DEG).astype(BF16)]
    ppermute x8 -> x0, waiting for transfers between devices: 9.07 us -> none  [shift(): lax.ppermute(x, 'patch', [(i, (i + (1 if up else -1)) % n) for i in range...]
    ppermute x8 -> x0, starting transfers between devices: 8.94 us -> none  [shift(): lax.ppermute(x, 'patch', [(i, (i + (1 if up else -1)) % n) for i in range...]
    convert_element_type x4 -> x0, other arithmetic: 3.49 us -> none  [the longest x2 2.78 us: local(): grad_pre = (grad_mean[None] * d_proc).astype(BF16)]
  transfers between devices with their start and end apart: 10 -> 0, of which waited for: 8 -> 0; matrix products, arithmetic and copies ran while one was open for 5% -> 0% of each run, Pallas kernels for 0% -> 0%
where the time goes in v1:
time: 78.2 us; the launch traced here: 78 us
  Pallas kernels  71.2 us (91%)
  local copies, waits for them, and re-layouts  6.15 us (8%)
    pallas_call x1, Pallas kernels, local(): pl.pallas_call(kernel, out_shape=(jax.ShapeDtypeStruct((nodes, width), BF...  71.2 us
    unnamed x3, local copies, waits for them, and re-layouts  4.89 us

profile of v1, /device:TPU:1, one launch (start us, length us, event | category | flops | bytes accessed | tf_op | source)
XLA Modules:
  0.0 78.0 jit_solution(3044514553986093869)
XLA Ops:
  0.6 1.3 %reshape.9.edge_vec = bf16[1,512]{1,0:T(2,128)(2,1)} reshape(bf16[512]{0:T(512)(128)(2,1)} %param.23) | data formatting | bytes 2048 | tf_op jit(solution)/shard_map/reshape | solution.py:384
  1.9 71.2 %shard_map.148 = (bf16[256,512]{1,0:T(8,128)(2,1)}, bf16[256,512]{1,0:T(8,128)(2,1)}, bf16[227,256]{1,0:T(8,128)(2,1)}) custom-call(bf16[227,256]{1,0:T(8,128)(2,1)} %bitcast.7, s32[4,256]{1,0:T(4,128)} %bitcast.9, s32[4,256]{1,0:T(4,128)} %bitcast.10, bf16[4,256]{1,0:T(4,128)(2,1)} %bitcast.11, s32[6,256]{1,0:T(8,128)} %bitcast.8, ...), custom_call_target="tpu_custom_call" | custom-call | tf_op jit(solution)/shard_map/pallas_call | solution.py:348
  73.1 1.7 %copy.19 = bf16[256,512]{1,0:T(8,128)(2,1)} copy(bf16[256,512]{1,0:T(8,128)(2,1)} %get-tuple-element.12) | data formatting | bytes 524288
  74.7 1.7 %copy.20 = bf16[256,512]{1,0:T(8,128)(2,1)} copy(bf16[256,512]{1,0:T(8,128)(2,1)} %get-tuple-element.13) | data formatting | bytes 524288
  76.4 1.6 %copy.21 = bf16[256,227]{0,1:T(8,128)(2,1)} copy(bf16[256,227]{0,1:T(8,128)(2,1)} %bitcast.6) | data formatting | bytes 232448

commit v2 on v1

--- a/solution.py
+++ b/solution.py
@@ -44,9 +44,9 @@
     return jnp.where(mask, 1.0, 0.0).astype(BF16)
 
 
-def offsets(slot):
-    dp = slot % 8
-    return (slot // 8 + 5 * dp) % 16, dp
+def wrap(value, size):
+    value = jnp.where(value >= 2 * size, value - 2 * size, value)
+    return jnp.where(value >= size, value - size, value)
 
 
 def kernel(
@@ -66,7 +66,7 @@
     nodes, width = state.shape
     cin, rows = feat_t.shape
     b, p = lax.axis_index("band"), lax.axis_index("patch")
-    left, right = (p + patches - 1) % patches, (p + 1) % patches
+    left, right = wrap(p + patches - 1, patches), wrap(p + 1, patches)
 
     loads = [
         pltpu.make_async_copy(src, dst, load_sem.at[i])
@@ -79,16 +79,10 @@
 
     barrier = pltpu.get_barrier_semaphore()
 
-    def greet_patch(i, carry):
-        pl.semaphore_signal(barrier, inc=1, device_id=(b, (p + i) % patches), device_id_type=pl.DeviceIdType.MESH)
-        return carry
-
-    def greet_band(i, carry):
-        pl.semaphore_signal(barrier, inc=1, device_id=((b + i) % bands, p), device_id_type=pl.DeviceIdType.MESH)
-        return carry
-
-    lax.fori_loop(1, patches, greet_patch, 0)
-    lax.fori_loop(1, bands, greet_band, 0)
+    for i in range(1, bands):
+        pl.semaphore_signal(barrier, inc=1, device_id=(wrap(b + i, bands), p), device_id_type=pl.DeviceIdType.MESH)
+    for i in range(1, patches):
+        pl.semaphore_signal(barrier, inc=1, device_id=(b, wrap(p + i, patches)), device_id_type=pl.DeviceIdType.MESH)
 
     meta[...] = jnp.zeros_like(meta)
     dest = dest_t[...]
@@ -119,38 +113,36 @@
         send_buf[pl.ds(pl.multiple_of(g * ROWS, ROWS), ROWS), :] = mm(pick_group(g), packed[...]).astype(BF16)
         return carry
 
-    lax.fori_loop(0, groups, fill, 0)
-
+    lax.fori_loop(0, groups // 2, fill, 0)
     pl.semaphore_wait(barrier, patches + bands - 2)
-
-    def greet_again(i, carry):
-        pl.semaphore_signal(entered, inc=1, device_id=((b + i) % bands, p), device_id_type=pl.DeviceIdType.MESH)
-        return carry
-
-    lax.fori_loop(1, bands, greet_again, 0)
+    for i in range(1, bands):
+        pl.semaphore_signal(entered, inc=1, device_id=(wrap(b + i, bands), p), device_id_type=pl.DeviceIdType.MESH)
+    lax.fori_loop(groups // 2, groups, fill, 0)
     pl.semaphore_wait(entered, bands - 1)
 
-    def block(t):
-        return pl.ds(pl.multiple_of(t * CAP, CAP), CAP)
-
-    def send_fwd(t, carry):
-        db, dp = offsets(t)
-        pltpu.make_async_remote_copy(
-            send_buf.at[block(t), :], recv_buf.at[block(t), :], fwd_send, fwd_recv.at[t // GROUP],
-            device_id=((b + db) % bands, (p + dp) % patches), device_id_type=pl.DeviceIdType.MESH,
-        ).start()
-        return carry
-
-    def send_bwd(t, carry):
-        db, dp = offsets(t)
-        pltpu.make_async_remote_copy(
-            back_buf.at[block(t), :], ret_buf.at[block(t), :], bwd_send, bwd_recv.at[t // GROUP],
-            device_id=((b + bands - db) % bands, (p + patches - dp) % patches), device_id_type=pl.DeviceIdType.MESH,
-        ).start()
-        return carry
-
+    def send_group(g, forward, first):
+        source, target = (send_buf, recv_buf) if forward else (back_buf, ret_buf)
+        sent, received = (fwd_send, fwd_recv) if forward else (bwd_send, bwd_recv)
+        for u in range(first, GROUP):
+            dp = u % patches
+            db = 2 * g + (u // patches + 5 * dp) % bands
+            if forward:
+                device = (wrap(b + db, bands), wrap(p + dp, patches))
+            else:
+                device = (wrap(b + 3 * bands - db, bands), wrap(p + patches - dp, patches))
+            rows_at = pl.ds(pl.multiple_of(g * ROWS + u * CAP, CAP), CAP)
+            pltpu.make_async_remote_copy(
+                source.at[rows_at, :], target.at[rows_at, :], sent, received.at[g],
+                device_id=device, device_id_type=pl.DeviceIdType.MESH,
+            ).start()
+
+    def send_more(g, carry):
+        send_group(g, True, 0)
+        return carry
+
+    send_group(0, True, 1)
     pltpu.make_async_copy(send_buf.at[pl.ds(0, CAP), :], recv_buf.at[pl.ds(0, CAP), :], fwd_recv.at[0]).start()
-    lax.fori_loop(1, peers, send_fwd, 0)
+    lax.fori_loop(1, groups, send_more, 0)
 
     w_emb[...] = jnp.zeros_like(w_emb)
     w_emb[0:cin, :] = w_embed[...]
@@ -203,7 +195,7 @@
     select = onehot((sel_k < TOP) & (sel_c == c0 + sel_k + TOP * lax.shift_right_logical(sel_l, 7)))
     select_t = onehot(iota((16, 128), 1) == c0 + iota((16, 128), 0))
     ones = jnp.ones((128, nodes), BF16)
-    edges = jnp.broadcast_to(edge_vec[...].astype(F32), (128, width)).astype(BF16)
+    edges = jnp.broadcast_to(edge_vec[...].astype(F32)[None, :], (128, width)).astype(BF16)
     acc[...] = jnp.zeros_like(acc)
 
     def encode(g, carry):
@@ -294,17 +286,21 @@
     agg = mm((grad[...] * d_node[...]).astype(BF16), w_node_t[...]).astype(BF16)
     recv_proj[...] = agg
 
-    def decode(g, carry):
+    def decode(g, first):
         at = pl.ds(pl.multiple_of(g * ROWS, ROWS), ROWS)
         edge = (mm(here[at, :], recv_proj[...]) * d_enc[at, :].astype(F32)).astype(BF16)
         d_enc[at, :] = edge
         emb = (mm(edge, w_send_t[...]) * d_emb[at, :].astype(F32)).astype(BF16)
         back_buf[at, :] = mm(emb, w_emb_t[...]).astype(BF16)
-        lax.fori_loop(jnp.maximum(g * GROUP, 1), (g + 1) * GROUP, send_bwd, 0)
-        return carry
-
-    lax.fori_loop(0, groups, decode, 0)
+        send_group(g, False, first)
+
+    def decode_more(g, carry):
+        decode(g, 0)
+        return carry
+
+    decode(0, 1)
     pltpu.make_async_copy(back_buf.at[pl.ds(0, CAP), :], ret_buf.at[pl.ds(0, CAP), :], bwd_recv.at[0]).start()
+    lax.fori_loop(1, groups, decode_more, 0)
     acc[...] = jnp.zeros_like(acc)
 
     def scatter(g, carry):
@@ -348,9 +344,9 @@
     mesh_out, mesh_grad, grid_grad_t = pl.pallas_call(
         kernel,
         out_shape=(
-            jax.ShapeDtypeStruct((nodes, width), BF16),
-            jax.ShapeDtypeStruct((nodes, width), BF16),
-            jax.ShapeDtypeStruct((cin, rows), BF16),
+            pltpu.VMEM((nodes, width), BF16),
+            pltpu.VMEM((nodes, width), BF16),
+            pltpu.VMEM((cin, rows), BF16),
         ),
         in_specs=[vmem] * 7 + [anywhere] * 6,
         out_specs=(vmem,) * 3,
@@ -381,7 +377,7 @@
             collective_id=0, has_side_effects=True, vmem_limit_bytes=56 * 2**20
         ),
     )(
-        grid_feat.T, g2m_dest.T, g2m_node.T, g2m_dist.T, mesh_src.T, w_embed, edge_vec.reshape(1, width),
+        grid_feat.T, g2m_dest.T, g2m_node.T, g2m_dist.T, mesh_src.T, w_embed, edge_vec,
         mesh_state, w_send, w_recv, w_node, proc_weights, cotangent,
     )
     return mesh_out, mesh_grad, grid_grad_t.T

time: 78.2 us -> 71.9 us (0.919)
  local copies, waits for them, and re-layouts: 6.15 us -> 2.05 us
  Pallas kernels: 71.2 us -> 69.1 us
    unnamed x3, local copies, waits for them, and re-layouts: 4.89 us -> 2.05 us
    pallas_call x1, Pallas kernels: 71.2 us -> 69.1 us  [local(): pl.pallas_call(kernel, out_shape=(pltpu.VMEM((nodes, width), BF16), pltpu...]
    reshape x1 -> x0, local copies, waits for them, and re-layouts: 1.26 us -> none  [local(): edge_vec.reshape(1, width)]
where the time goes in v2:
time: 71.9 us; the launch traced here: 71.8 us
  Pallas kernels  69.1 us (96%)
  local copies, waits for them, and re-layouts  2.05 us (3%)
    pallas_call x1, Pallas kernels, local(): pl.pallas_call(kernel, out_shape=(pltpu.VMEM((nodes, width), BF16), pltpu...  69.1 us
    unnamed x3, local copies, waits for them, and re-layouts  2.05 us

profile of v2, /device:TPU:1, one launch (start us, length us, event | category | flops | bytes accessed | tf_op | source)
XLA Modules:
  0.0 71.8 jit_solution(4122763775130580276)
XLA Ops:
  0.6 69.1 %shard_map.148 = (bf16[256,512]{1,0:T(8,128)(2,1)S(1)}, bf16[256,512]{1,0:T(8,128)(2,1)S(1)}, bf16[227,256]{1,0:T(8,128)(2,1)S(1)}) custom-call(bf16[227,256]{1,0:T(8,128)(2,1)} %bitcast.7, s32[4,256]{1,0:T(4,128)} %bitcast.9, s32[4,256]{1,0:T(4,128)} %bitcast.10, bf16[4,256]{1,0:T(4,128)(2,1)} %bitcast.11, s32[6,256]{1,0:T(8,128)} %bitcast.8, ...), custom_call_target="tpu_custom_call" | custom-call | tf_op jit(solution)/shard_map/pallas_call | solution.py:344
  69.7 0.7 copy.19
  70.4 0.6 copy.21
  71.1 0.7 copy.20

commit v3 on v2

--- a/solution.py
+++ b/solution.py
@@ -50,9 +50,10 @@
 
 
 def kernel(
-    feat_t, dest_t, node_t, dist_t, src_t, w_embed, edge_vec,
+    feat_hbm, dest_hbm, node_hbm, dist_hbm, src_hbm, embed_hbm, edge_hbm,
     state_hbm, w_send_hbm, w_recv_hbm, w_node_hbm, proc_hbm, cot_hbm,
     mesh_out, mesh_grad, grid_grad_t,
+    feat_t, dest_t, node_t, dist_t, src_t, w_embed, edge_vec,
     state, w_send, w_recv, w_node, proc, cot, w_emb,
     w_send_t, w_recv_t, w_node_t, proc_t, w_emb_t,
     meta, packed_t, packed, place, send_buf, recv_buf, back_buf, ret_buf, unpick,
@@ -71,11 +72,13 @@
     loads = [
         pltpu.make_async_copy(src, dst, load_sem.at[i])
         for i, (src, dst) in enumerate(
-            [(state_hbm, state), (w_recv_hbm, w_recv), (w_send_hbm, w_send), (w_node_hbm, w_node), (proc_hbm, proc), (cot_hbm, cot)]
+            [
+                (state_hbm, state), (w_recv_hbm, w_recv), (w_send_hbm, w_send), (w_node_hbm, w_node), (proc_hbm, proc), (cot_hbm, cot),
+                (feat_hbm, feat_t), (dest_hbm, dest_t), (node_hbm, node_t), (dist_hbm, dist_t), (src_hbm, src_t), (embed_hbm, w_embed),
+                (edge_hbm, edge_vec),
+            ]
         )
     ]
-    for load in loads:
-        load.start()
 
     barrier = pltpu.get_barrier_semaphore()
 
@@ -83,6 +86,11 @@
         pl.semaphore_signal(barrier, inc=1, device_id=(wrap(b + i, bands), p), device_id_type=pl.DeviceIdType.MESH)
     for i in range(1, patches):
         pl.semaphore_signal(barrier, inc=1, device_id=(b, wrap(p + i, patches)), device_id_type=pl.DeviceIdType.MESH)
+
+    for load in loads[6:] + loads[:6]:
+        load.start()
+    for load in loads[6:]:
+        load.wait()
 
     meta[...] = jnp.zeros_like(meta)
     dest = dest_t[...]
@@ -110,20 +118,21 @@
         return onehot(slot_place == (iota((ROWS, rows), 0) & (CAP - 1)).astype(F32))
 
     def fill(g, carry):
-        send_buf[pl.ds(pl.multiple_of(g * ROWS, ROWS), ROWS), :] = mm(pick_group(g), packed[...]).astype(BF16)
-        return carry
-
-    lax.fori_loop(0, groups // 2, fill, 0)
+        for i in range(2):
+            at = pl.multiple_of((2 * g + i) * ROWS, ROWS)
+            send_buf[pl.ds(at, ROWS), :] = mm(pick_group(2 * g + i), packed[...]).astype(BF16)
+        return carry
+
+    lax.fori_loop(0, 2, fill, 0)
     pl.semaphore_wait(barrier, patches + bands - 2)
     for i in range(1, bands):
         pl.semaphore_signal(entered, inc=1, device_id=(wrap(b + i, bands), p), device_id_type=pl.DeviceIdType.MESH)
-    lax.fori_loop(groups // 2, groups, fill, 0)
-    pl.semaphore_wait(entered, bands - 1)
-
-    def send_group(g, forward, first):
+    lax.fori_loop(2, 4, fill, 0)
+
+    def send_group(g, forward, which):
         source, target = (send_buf, recv_buf) if forward else (back_buf, ret_buf)
         sent, received = (fwd_send, fwd_recv) if forward else (bwd_send, bwd_recv)
-        for u in range(first, GROUP):
+        for u in which:
             dp = u % patches
             db = 2 * g + (u // patches + 5 * dp) % bands
             if forward:
@@ -137,10 +146,19 @@
             ).start()
 
     def send_more(g, carry):
-        send_group(g, True, 0)
-        return carry
-
-    send_group(0, True, 1)
+        send_group(g, True, others)
+        return carry
+
+    def send_column(g, carry):
+        send_group(g, True, column)
+        return carry
+
+    column = (0, patches)
+    others = [u for u in range(GROUP) if u not in column]
+    send_group(0, True, column[1:])
+    lax.fori_loop(1, groups, send_column, 0)
+    pl.semaphore_wait(entered, bands - 1)
+    send_group(0, True, others)
     pltpu.make_async_copy(send_buf.at[pl.ds(0, CAP), :], recv_buf.at[pl.ds(0, CAP), :], fwd_recv.at[0]).start()
     lax.fori_loop(1, groups, send_more, 0)
 
@@ -286,19 +304,19 @@
     agg = mm((grad[...] * d_node[...]).astype(BF16), w_node_t[...]).astype(BF16)
     recv_proj[...] = agg
 
-    def decode(g, first):
+    def decode(g, which):
         at = pl.ds(pl.multiple_of(g * ROWS, ROWS), ROWS)
         edge = (mm(here[at, :], recv_proj[...]) * d_enc[at, :].astype(F32)).astype(BF16)
         d_enc[at, :] = edge
         emb = (mm(edge, w_send_t[...]) * d_emb[at, :].astype(F32)).astype(BF16)
         back_buf[at, :] = mm(emb, w_emb_t[...]).astype(BF16)
-        send_group(g, False, first)
+        send_group(g, False, which)
 
     def decode_more(g, carry):
-        decode(g, 0)
-        return carry
-
-    decode(0, 1)
+        decode(g, range(GROUP))
+        return carry
+
+    decode(0, range(1, GROUP))
     pltpu.make_async_copy(back_buf.at[pl.ds(0, CAP), :], ret_buf.at[pl.ds(0, CAP), :], bwd_recv.at[0]).start()
     lax.fori_loop(1, groups, decode_more, 0)
     acc[...] = jnp.zeros_like(acc)
@@ -325,9 +343,9 @@
 
     for swap in swaps:
         swap.wait_send()
-    others = pl.ds(CAP, (peers - 1) * CAP)
-    pltpu.make_async_copy(send_buf.at[others, :], send_buf.at[others, :], fwd_send).wait()
-    pltpu.make_async_copy(back_buf.at[others, :], back_buf.at[others, :], bwd_send).wait()
+    away = pl.ds(CAP, (peers - 1) * CAP)
+    pltpu.make_async_copy(send_buf.at[away, :], send_buf.at[away, :], fwd_send).wait()
+    pltpu.make_async_copy(back_buf.at[away, :], back_buf.at[away, :], bwd_send).wait()
 
 
 def local(grid_feat, mesh_state, g2m_dest, g2m_node, g2m_dist, mesh_src, w_embed, w_send, w_recv, w_node, edge_vec, proc_weights, cotangent):
@@ -348,9 +366,11 @@
             pltpu.VMEM((nodes, width), BF16),
             pltpu.VMEM((cin, rows), BF16),
         ),
-        in_specs=[vmem] * 7 + [anywhere] * 6,
+        in_specs=[anywhere] * 13,
         out_specs=(vmem,) * 3,
         scratch_shapes=[
+            pltpu.VMEM((cin, rows), BF16), pltpu.VMEM((TOP, rows), I32), pltpu.VMEM((TOP, rows), I32), pltpu.VMEM((TOP, rows), BF16),
+            pltpu.VMEM((DEG, nodes), I32), pltpu.VMEM((cin, width), BF16), pltpu.VMEM((width,), BF16),
             tile, square, square, square, stack, tile, pltpu.VMEM((WIDE, width), BF16),
             square, square, square, stack, pltpu.VMEM((width, WIDE), BF16),
             pltpu.VMEM((16, rows), F32), pltpu.VMEM((WIDE, rows), BF16), pltpu.VMEM((rows, WIDE), BF16),
@@ -367,7 +387,7 @@
             pltpu.VMEM((LAYERS, nodes, width), BF16), pltpu.VMEM((2 * nodes, width), BF16),
             pltpu.VMEM((DEG * nodes, width), BF16), pltpu.VMEM((LAYERS, 2 * RIM, width), BF16),
             pltpu.VMEM((nodes, width), F32), pltpu.VMEM((2 * LAYERS, 2, RIM, width), BF16),
-            pltpu.SemaphoreType.DMA((6,)),
+            pltpu.SemaphoreType.DMA((13,)),
             pltpu.SemaphoreType.DMA, pltpu.SemaphoreType.DMA((groups,)),
             pltpu.SemaphoreType.DMA, pltpu.SemaphoreType.DMA((groups,)),
             pltpu.SemaphoreType.DMA((2 * LAYERS, 2)), pltpu.SemaphoreType.DMA((2 * LAYERS, 2)),

time: 71.9 us -> 70.4 us (0.979)
  Pallas kernels: 69.1 us -> 67.6 us
    pallas_call x1, Pallas kernels: 69.1 us -> 67.6 us  [local(): pl.pallas_call(kernel, out_shape=(pltpu.VMEM((nodes, width), BF16), pltpu...]
where the time goes in v3:
time: 70.4 us; the launch traced here: 70.3 us
  Pallas kernels  67.6 us (96%)
  local copies, waits for them, and re-layouts  2.05 us (3%)
    pallas_call x1, Pallas kernels, local(): pl.pallas_call(kernel, out_shape=(pltpu.VMEM((nodes, width), BF16), pltpu...  67.6 us
    unnamed x3, local copies, waits for them, and re-layouts  2.05 us

profile of v3, /device:TPU:1, one launch (start us, length us, event | category | flops | bytes accessed | tf_op | source)
XLA Modules:
  0.0 70.3 jit_solution(3367404826063453032)
XLA Ops:
  0.6 67.6 %shard_map.148 = (bf16[256,512]{1,0:T(8,128)(2,1)S(1)}, bf16[256,512]{1,0:T(8,128)(2,1)S(1)}, bf16[227,256]{1,0:T(8,128)(2,1)S(1)}) custom-call(bf16[227,256]{1,0:T(8,128)(2,1)} %bitcast.7, s32[4,256]{1,0:T(4,128)} %bitcast.9, s32[4,256]{1,0:T(4,128)} %bitcast.10, bf16[4,256]{1,0:T(4,128)(2,1)} %bitcast.11, s32[6,256]{1,0:T(8,128)} %bitcast.8, ...), custom_call_target="tpu_custom_call" | custom-call | tf_op jit(solution)/shard_map/pallas_call | solution.py:362
  68.2 0.7 %copy.19 = bf16[256,512]{1,0:T(8,128)(2,1)} copy(bf16[256,512]{1,0:T(8,128)(2,1)S(1)} %get-tuple-element.9) | data formatting | bytes 524288
  68.9 0.6 copy.21
  69.6 0.7 copy.20

commit v4 on v3

--- a/solution.py
+++ b/solution.py
@@ -31,6 +31,13 @@
 
 
 def act(value):
+    sig = 0.5 * jnp.tanh(0.5 * value) + 0.5
+    out = value * sig
+    return out, sig + out * (1.0 - sig)
+
+
+def act_half(value):
+    value = value.astype(BF16)
     sig = 0.5 * jnp.tanh(0.5 * value) + 0.5
     out = value * sig
     return out, sig + out * (1.0 - sig)
@@ -272,9 +279,8 @@
         send_p[nodes + RIM : nodes + 2 * RIM, :] = mm(rims[layer, 1], proc[layer, 0]).astype(BF16)
         for k in range(DEG):
             at = slice(k * nodes, (k + 1) * nodes)
-            out, slope = act(recv_p + mm(chosen[at, :], send_p[...]))
-            d_proc[layer, at, :] = slope.astype(BF16)
-            acc[...] = out if k == 0 else acc[...] + out
+            out, d_proc[layer, at, :] = act_half(recv_p + mm(chosen[at, :], send_p[...]))
+            acc[...] = out.astype(F32) if k == 0 else acc[...] + out.astype(F32)
         upd, slope = act(mm((acc[...] * (1.0 / DEG)).astype(BF16), proc[layer, 2]))
         d_upd[layer] = slope
         after = (now.astype(F32) + upd).astype(BF16)

time: 70.4 us -> 69.9 us (level)
  no operation moved by 1% of the time
where the time goes in v4:
time: 69.9 us; the launch traced here: 69.8 us
  Pallas kernels  67.1 us (96%)
  local copies, waits for them, and re-layouts  2.05 us (3%)
    pallas_call x1, Pallas kernels, local(): pl.pallas_call(kernel, out_shape=(pltpu.VMEM((nodes, width), BF16), pltpu...  67.1 us
    unnamed x3, local copies, waits for them, and re-layouts  2.05 us

profile of v4, /device:TPU:1, one launch (start us, length us, event | category | flops | bytes accessed | tf_op | source)
XLA Modules:
  0.0 69.8 jit_solution(15740671081358670635)
XLA Ops:
  0.6 67.1 %shard_map.148 = (bf16[256,512]{1,0:T(8,128)(2,1)S(1)}, bf16[256,512]{1,0:T(8,128)(2,1)S(1)}, bf16[227,256]{1,0:T(8,128)(2,1)S(1)}) custom-call(bf16[227,256]{1,0:T(8,128)(2,1)} %bitcast.7, s32[4,256]{1,0:T(4,128)} %bitcast.9, s32[4,256]{1,0:T(4,128)} %bitcast.10, bf16[4,256]{1,0:T(4,128)(2,1)} %bitcast.11, s32[6,256]{1,0:T(8,128)} %bitcast.8, ...), custom_call_target="tpu_custom_call" | custom-call | tf_op jit(solution)/shard_map/pallas_call | solution.py:368
  67.8 0.7 %copy.19 = bf16[256,512]{1,0:T(8,128)(2,1)} copy(bf16[256,512]{1,0:T(8,128)(2,1)S(1)} %get-tuple-element.9) | data formatting | bytes 524288
  68.5 0.6 copy.21
  69.1 0.7 %copy.20 = bf16[256,512]{1,0:T(8,128)(2,1)} copy(bf16[256,512]{1,0:T(8,128)(2,1)S(1)} %get-tuple-element.10) | data formatting | bytes 524288

commit v5 on v4

--- a/solution.py
+++ b/solution.py
@@ -240,11 +240,9 @@
             node_row = node_row + jnp.where(fields_t[k : k + 1, :] == me1, fields_t[TOP + k : TOP + k + 1, :], 0.0)
         at_node_t = onehot(node_row == (iota((nodes, ROWS), 0) + 1).astype(F32))
         here_t[g] = at_node_t
-        latent, slope = act(mm(got, w_emb[...]))
-        d_emb[at, :] = slope.astype(BF16)
-        enc, slope = act(mm(latent.astype(BF16), w_send[...]) + mm(at_node, recv_proj[...]) + length)
-        d_enc[at, :] = slope.astype(BF16)
-        acc[...] += mm(at_node_t, enc.astype(BF16))
+        latent, d_emb[at, :] = act_half(mm(got, w_emb[...]))
+        enc, d_enc[at, :] = act_half(mm(latent, w_send[...]) + mm(at_node, recv_proj[...]) + length)
+        acc[...] += mm(at_node_t, enc)
         return carry
 
     lax.fori_loop(0, groups, encode, 0)

time: 69.9 us -> 69.6 us (level)
  no operation moved by 1% of the time
where the time goes in v5:
time: 69.6 us; the launch traced here: 69.5 us
  Pallas kernels  66.8 us (96%)
  local copies, waits for them, and re-layouts  2.05 us (3%)
    pallas_call x1, Pallas kernels, local(): pl.pallas_call(kernel, out_shape=(pltpu.VMEM((nodes, width), BF16), pltpu...  66.8 us
    unnamed x3, local copies, waits for them, and re-layouts  2.05 us

profile of v5, /device:TPU:1, one launch (start us, length us, event | category | flops | bytes accessed | tf_op | source)
XLA Modules:
  0.0 69.5 jit_solution(14918299653676431736)
XLA Ops:
  0.6 66.8 %shard_map.148 = (bf16[256,512]{1,0:T(8,128)(2,1)S(1)}, bf16[256,512]{1,0:T(8,128)(2,1)S(1)}, bf16[227,256]{1,0:T(8,128)(2,1)S(1)}) custom-call(bf16[227,256]{1,0:T(8,128)(2,1)} %bitcast.7, s32[4,256]{1,0:T(4,128)} %bitcast.9, s32[4,256]{1,0:T(4,128)} %bitcast.10, bf16[4,256]{1,0:T(4,128)(2,1)} %bitcast.11, s32[6,256]{1,0:T(8,128)} %bitcast.8, ...), custom_call_target="tpu_custom_call" | custom-call | tf_op jit(solution)/shard_map/pallas_call | solution.py:366
  67.4 0.7 %copy.19 = bf16[256,512]{1,0:T(8,128)(2,1)} copy(bf16[256,512]{1,0:T(8,128)(2,1)S(1)} %get-tuple-element.9) | data formatting | bytes 524288
  68.1 0.6 copy.21
  68.8 0.7 %copy.20 = bf16[256,512]{1,0:T(8,128)(2,1)} copy(bf16[256,512]{1,0:T(8,128)(2,1)S(1)} %get-tuple-element.10) | data formatting | bytes 524288

commit v6 on v5

--- a/solution.py
+++ b/solution.py
@@ -245,7 +245,11 @@
         acc[...] += mm(at_node_t, enc)
         return carry
 
-    lax.fori_loop(0, groups, encode, 0)
+    def encode_two(i, carry):
+        encode(2 * i, carry)
+        return encode(2 * i + 1, carry)
+
+    lax.fori_loop(0, groups // 2, encode_two, 0)
 
     upd, slope = act(mm(acc[...].astype(BF16), w_node[...]))
     d_node[...] = slope

time: 69.6 us -> 69.4 us (level)
  no operation moved by 1% of the time
where the time goes in v6:
time: 69.4 us; the launch traced here: 69.3 us
  Pallas kernels  66.6 us (96%)
  local copies, waits for them, and re-layouts  2.05 us (3%)
    pallas_call x1, Pallas kernels, local(): pl.pallas_call(kernel, out_shape=(pltpu.VMEM((nodes, width), BF16), pltpu...  66.6 us
    unnamed x3, local copies, waits for them, and re-layouts  2.05 us

profile of v6, /device:TPU:1, one launch (start us, length us, event | category | flops | bytes accessed | tf_op | source)
XLA Modules:
  0.0 69.3 jit_solution(2428106902863546076)
XLA Ops:
  0.6 66.6 %shard_map.148 = (bf16[256,512]{1,0:T(8,128)(2,1)S(1)}, bf16[256,512]{1,0:T(8,128)(2,1)S(1)}, bf16[227,256]{1,0:T(8,128)(2,1)S(1)}) custom-call(bf16[227,256]{1,0:T(8,128)(2,1)} %bitcast.7, s32[4,256]{1,0:T(4,128)} %bitcast.9, s32[4,256]{1,0:T(4,128)} %bitcast.10, bf16[4,256]{1,0:T(4,128)(2,1)} %bitcast.11, s32[6,256]{1,0:T(8,128)} %bitcast.8, ...), custom_call_target="tpu_custom_call" | custom-call | tf_op jit(solution)/shard_map/pallas_call | solution.py:370
  67.3 0.7 %copy.19 = bf16[256,512]{1,0:T(8,128)(2,1)} copy(bf16[256,512]{1,0:T(8,128)(2,1)S(1)} %get-tuple-element.9) | data formatting | bytes 524288
  68.0 0.6 copy.21
  68.6 0.7 %copy.20 = bf16[256,512]{1,0:T(8,128)(2,1)} copy(bf16[256,512]{1,0:T(8,128)(2,1)S(1)} %get-tuple-element.10) | data formatting | bytes 524288
